TPU v7x, 128 devices: a whole 4x4x4 slice. The times are simulated.
128 devices in a mesh: rows: 32 (over y, x_lo, z), protos: 4 (over x_hi, core).
Axes of the slice: x: 4 (x_hi: 2, x_lo: 2; x = x_hi * 2 + x_lo), y: 4, z: 4, core: 2. Of those that a mesh axis runs over, the one named last changes fastest.
Arguments:
- student: bfloat16 [16384, 256], P('rows'), may hold values from -256 to 256
- teacher: bfloat16 [16384, 256], P('rows'), may hold values from -256 to 256
- prototypes: bfloat16 [65536, 256], P('protos'), may hold values from -1 to 1
- masked: int32 [16384], P('rows'), may hold values from 0 to 1, as said below
Outputs:
- feature_grad: bfloat16 [16384, 256], P(('rows', 'protos'))
- proto_grad: bfloat16 [65536, 256], P(('protos', 'rows'))
Inputs may be any that keep to these rules, and one draw needn't show every extreme that they name: Rows whose index is a multiple of 16 are masked.
All inputs are finite; a program needn't handle non-finite values.
Results may differ from a plain program's by a relative error of at most 0.02.
Values may be sent and summed in bfloat16 or wider, within the bound.
No kernel may reach another device: no remote copies, remote signals or barrier semaphores. Data moves between devices by JAX's collectives and lax.ppermute only.
A program may use at most 256 MiB of HBM per device.

v0:
```python
import math

import jax
import jax.numpy as jnp
from jax import lax
from jax.sharding import PartitionSpec as P

ITERS = 3


student_temp = 0.1
teacher_temp = 0.05


def column_step(weights, expo, proto_total):
    partial_value = jnp.dot(weights, expo, precision=lax.Precision.HIGHEST)
    colsum = lax.psum(partial_value.astype(jnp.bfloat16), "rows").astype(jnp.float32)
    return 1.0 / (proto_total * colsum)


def row_step(col_scale, expo, row_keep):
    partial_value = jnp.dot(expo, col_scale, precision=lax.Precision.HIGHEST)
    rowsum = lax.psum(partial_value, "protos")
    return row_keep / jnp.where(row_keep > 0, rowsum, 1.0)


def local(student, teacher, prototypes, masked):
    proto_local = prototypes.shape[0]
    proto_parts = lax.axis_size("protos")
    proto_total = proto_local * proto_parts
    row_keep = masked.astype(jnp.float32)
    teach_logit = (
        jnp.einsum("rd,kd->rk", teacher, prototypes, preferred_element_type=jnp.float32)
        / teacher_temp
    )
    stud_logit = (
        jnp.einsum("rd,kd->rk", student, prototypes, preferred_element_type=jnp.float32)
        / student_temp
    )
    teach_max, stud_max = lax.pmax(
        (jnp.max(teach_logit, axis=1), jnp.max(stud_logit, axis=1)), "protos"
    )
    expo = row_keep[:, None] * jnp.exp(teach_logit - teach_max[:, None])
    stud_exp = jnp.exp(stud_logit - stud_max[:, None])
    local_total = jnp.sum(stud_exp, axis=1)
    local_count = jnp.sum(row_keep)
    weights = row_keep
    mask_total = lax.psum(local_count, "rows")
    soft_total = lax.psum(local_total, "protos")
    col_scale = column_step(weights, expo, proto_total)
    weights = row_step(col_scale, expo, row_keep)
    for iteration in range(1, ITERS):
        col_scale = column_step(weights, expo, proto_total)
        weights = row_step(col_scale, expo, row_keep)
    plan = weights[:, None] * expo * col_scale[None, :]
    probs = stud_exp / soft_total[:, None]
    grad_logit = (row_keep[:, None] * (proto_total * (probs - plan))).astype(jnp.bfloat16)
    piece = grad_logit
    feature_sum = lax.psum_scatter(
        jnp.dot(piece, prototypes, preferred_element_type=jnp.float32).astype(jnp.bfloat16),
        "protos",
        scatter_dimension=0,
        tiled=True,
    ).astype(jnp.float32)
    feature_grad = (feature_sum / (student_temp * math.sqrt(proto_total))).astype(jnp.bfloat16)
    piece = grad_logit
    proto_sum = lax.psum_scatter(
        jnp.einsum("rk,rd->kd", piece, student, preferred_element_type=jnp.float32),
        "rows",
        scatter_dimension=0,
        tiled=True,
    )
    proto_grad = (proto_sum / jnp.sqrt(mask_total)).astype(jnp.bfloat16)
    return (feature_grad, proto_grad)


def solution(mesh):
    in_specs = (P("rows", None), P("rows", None), P("protos", None), P("rows"))
    out_specs = (P(("rows", "protos"), None), P(("protos", "rows"), None))
    return jax.shard_map(local, mesh=mesh, in_specs=in_specs, out_specs=out_specs, check_vma=False)
```

profile of v0, /device:TPU:0, one launch (start us, length us, event | category | flops | bytes accessed | tf_op | source)
XLA Modules:
  0.0 1009.8 jit_solution(17300995906483484947)
XLA Ops:
  7.2 0.0 copy-start
  7.2 0.0 reduce-scatter.3.cloned.1.call-start
  7.2 0.9 copy-done
  8.1 16.5 %multiply_reduce_fusion.1 = (f32[512]{0:T(512)S(1)}, f32[512,16384]{1,0:T(8,128)}) fusion(bf16[512,256]{1,0:T(8,128)(2,1)S(1)} %copy-done, bf16[16384,256]{1,0:T(8,128)(2,1)} %param.6), kind=kOutput, calls=%fused_computation.4 | convolution fusion | flops 4311744000 | bytes 42207232 | tf_op jit(solution)/shard_map/rd,kd->rk/dot_general | solution.py:37
  24.6 16.5 %multiply_reduce_fusion = (f32[512]{0:T(512)S(1)}, f32[512,16384]{1,0:T(8,128)}) fusion(bf16[512,256]{1,0:T(8,128)(2,1)S(1)} %copy-done.1, bf16[16384,256]{1,0:T(8,128)(2,1)} %param.6), kind=kOutput, calls=%fused_computation.3 | convolution fusion | flops 4311744000 | bytes 42207232 | tf_op jit(solution)/shard_map/rd,kd->rk/dot_general | solution.py:33
  41.1 10.0 all-reduce.1
  51.1 24.1 %exponential_multiply_fusion = f32[512,16384]{1,0:T(8,128)} fusion(f32[512,16384]{1,0:T(8,128)} %get-tuple-element.10, f32[512]{0:T(512)S(1)} %get-tuple-element.4, f32[512]{0:T(512)S(1)} %convert_element_type.36), kind=kLoop, calls=%fused_computation.1 | loop fusion | flops 25165824 | bytes 67112960 | tf_op jit(solution)/shard_map/mul | solution.py:43
  75.1 21.1 %fusion.1 = f32[1,16384]{1,0:T(1,128)S(1)} fusion(f32[512,16384]{1,0:T(8,128)} %exponential_multiply_fusion, f32[512,1]{0,1:T(1,128)S(1)} %bitcast.38), kind=kOutput, calls=%fused_computation.18 | convolution fusion | flops 100663296 | bytes 33622016 | tf_op jit(solution)/shard_map/dot_general | solution.py:16
  96.2 158.8 %psum.57 = bf16[16384]{0:T(1024)(128)(2,1)S(1)} all-reduce(bf16[16384]{0:T(1024)(128)(2,1)S(1)} %convert_element_type.37), channel_id=1, replica_groups=mesh['rows'=32,'protos'=4] {'rows'}, use_global_device_ids=true, to_apply=%region_6.0 | all-reduce | flops 16384 | bytes 65536 | tf_op jit(solution)/shard_map/psum | solution.py:17
  255.0 31.9 %fusion.2 = f32[1,512]{1,0:T(1,128)S(1)} fusion(f32[512,16384]{1,0:T(8,128)} %exponential_multiply_fusion, f32[16384,1]{0,1:T(1,128)S(1)} %bitcast.34), kind=kOutput, calls=%fused_computation.19 | convolution fusion | flops 100663296 | bytes 33622016 | tf_op jit(solution)/shard_map/dot_general | solution.py:22
  286.9 7.2 psum.58
  294.0 0.6 convert_reduce_fusion
  294.6 19.5 %fusion.3 = f32[1,16384]{1,0:T(1,128)S(1)} fusion(f32[512,1]{0,1:T(1,128)S(1)} %bitcast.39, f32[512,16384]{1,0:T(8,128)} %exponential_multiply_fusion), kind=kOutput, calls=%fused_computation.20 | convolution fusion | flops 100663296 | bytes 33622016 | tf_op jit(solution)/shard_map/dot_general | solution.py:16
  314.2 152.3 %psum.59 = bf16[16384]{0:T(1024)(128)(2,1)S(1)} all-reduce(bf16[16384]{0:T(1024)(128)(2,1)S(1)} %convert_element_type.39), channel_id=1, replica_groups=mesh['rows'=32,'protos'=4] {'rows'}, use_global_device_ids=true, to_apply=%region_8.0 | all-reduce | flops 16384 | bytes 65536 | tf_op jit(solution)/shard_map/psum | solution.py:17
  466.5 31.9 %fusion.4 = f32[1,512]{1,0:T(1,128)S(1)} fusion(f32[512,16384]{1,0:T(8,128)} %exponential_multiply_fusion, f32[16384,1]{0,1:T(1,128)S(1)} %bitcast.36), kind=kOutput, calls=%fused_computation.21 | convolution fusion | flops 100663296 | bytes 33622016 | tf_op jit(solution)/shard_map/dot_general | solution.py:22
  498.4 7.2 psum.60
  505.5 19.5 %fusion.5 = f32[1,16384]{1,0:T(1,128)S(1)} fusion(f32[512,1]{0,1:T(1,128)S(1)} %bitcast.40, f32[512,16384]{1,0:T(8,128)} %exponential_multiply_fusion), kind=kOutput, calls=%fused_computation.22 | convolution fusion | flops 100663296 | bytes 33622016 | tf_op jit(solution)/shard_map/dot_general | solution.py:16
  525.1 152.5 %psum.61 = bf16[16384]{0:T(1024)(128)(2,1)S(1)} all-reduce(bf16[16384]{0:T(1024)(128)(2,1)S(1)} %convert_element_type.41), channel_id=1, replica_groups=mesh['rows'=32,'protos'=4] {'rows'}, use_global_device_ids=true, to_apply=%region_10.11 | all-reduce | flops 16384 | bytes 65536 | tf_op jit(solution)/shard_map/psum | solution.py:17
  677.6 31.9 %fusion.6 = f32[1,512]{1,0:T(1,128)S(1)} fusion(f32[512,16384]{1,0:T(8,128)} %exponential_multiply_fusion, f32[16384,1]{0,1:T(1,128)S(1)} %bitcast.32), kind=kOutput, calls=%fused_computation.23 | convolution fusion | flops 100663296 | bytes 33622016 | tf_op jit(solution)/shard_map/dot_general | solution.py:22
  709.5 14.1 %fusion = f32[512]{0:T(512)S(1)} fusion(f32[512,16384]{1,0:T(8,128)} %get-tuple-element.12, f32[512]{0:T(512)S(1)} %get-tuple-element.5), kind=kLoop, calls=%fused_computation.5 | loop fusion | flops 25165312 | bytes 33558528 | tf_op jit(solution)/shard_map/reduce_sum | solution.py:45
  723.5 7.3 all-reduce
  730.9 28.3 %multiply_convert_fusion = bf16[512,16384]{1,0:T(8,128)(2,1)} fusion(f32[512,16384]{1,0:T(8,128)} %get-tuple-element.12, f32[512]{0:T(512)S(1)} %get-tuple-element.8, f32[16384]{0:T(1024)S(1)} %multiply_divide_fusion, f32[512]{0:T(512)S(1)} %select_divide_fusion, f32[512]{0:T(512)S(1)} %get-tuple-element.3, f32[512]{0:T(512)S(1)} %get-tuple-element.5, ...), kind=kLoop, calls=%fused_computation | loop fusion | flops 92274688 | bytes 83963904 | tf_op jit(solution)/shard_map/convert_element_type | solution.py:57
  759.2 13.3 %convolution_convert_fusion = bf16[512,256]{1,0:T(8,128)(2,1)} fusion(bf16[512,16384]{1,0:T(8,128)(2,1)} %multiply_convert_fusion, bf16[16384,256]{1,0:T(8,128)(2,1)} %param.6), kind=kOutput, calls=%fused_computation.6 | convolution fusion | flops 4295098368 | bytes 25427968 | tf_op jit(solution)/shard_map/dot_general | solution.py:60
  772.5 0.0 reduce-scatter.3.cloned.1.call-update
  772.5 0.0 reduce-scatter.5.cloned.1.call-start
  772.6 16.2 %fusion.7 = f32[16384,256]{1,0:T(8,128)} fusion(bf16[512,16384]{1,0:T(8,128)(2,1)} %multiply_convert_fusion, bf16[512,256]{1,0:T(8,128)(2,1)S(1)} %copy-done), kind=kOutput, calls=%fused_computation.24 | convolution fusion | flops 4294967296 | bytes 33816576 | tf_op jit(solution)/shard_map/rk,rd->kd/dot_general | solution.py:68
  788.8 0.0 reduce-scatter.5.cloned.1.call-update
  788.8 78.1 %psum.63 = f32[]{:T(128)} all-reduce(f32[]{:T(128)} %get-tuple-element.6), channel_id=1, replica_groups=mesh['rows'=32,'protos'=4] {'rows'}, use_global_device_ids=true, to_apply=%region_15.16 | all-reduce | flops 1 | bytes 8 | tf_op jit(solution)/shard_map/psum | solution.py:48
  867.6 0.0 reduce-scatter.3.cloned.1.call-done
  867.6 1.5 multiply_convert_fusion.1
  869.1 131.9 %reduce-scatter.5.cloned.1.call-done = f32[512,256]{1,0:T(8,128)} async-done(((f32[16384,256]{1,0:T(8,128)}), f32[512,256]{1,0:T(8,128)}) %reduce-scatter.5.cloned.1.call-update) | async-done | bytes 524304 | tf_op jit(solution)/shard_map/reduce_scatter | solution.py:67
  1001.0 1.8 divide_convert_fusion
  (13 shorter events, 0.1 us)
Async XLA Ops:
  7.2 1.0 copy-start
  7.2 17.4 %copy-start.1 = (bf16[512,256]{1,0:T(8,128)(2,1)S(1)}, bf16[512,256]{1,0:T(8,128)(2,1)}, u32[]{:S(2)}) copy-start(bf16[512,256]{1,0:T(8,128)(2,1)} %param.5) | copy-start | bytes 786436
  7.2 33.9 %copy-start.2 = (s32[512]{0:T(512)S(1)}, s32[512]{0:T(512)}, u32[]{:S(2)}) copy-start(s32[512]{0:T(512)} %param.7) | copy-start | bytes 6148
  7.2 860.4 %reduce-scatter.3.cloned.1.call-start = ((), (), s32[]{:S(2)}) async-start(), calls=%async_computation.2 | async-start | bytes 327680 | tf_op jit(solution)/shard_map/reduce_scatter | solution.py:59
  772.5 228.5 %reduce-scatter.5.cloned.1.call-start = ((), (), s32[]{:S(2)}) async-start(), calls=%async_computation.3 | async-start | bytes 17301504 | tf_op jit(solution)/shard_map/reduce_scatter | solution.py:67
Sparse Core Ops, SparseCore 0:
  772.7 22.2 reduce-scatter.2
  797.5 203.4 reduce-scatter.4
where the time goes:
time: 1020 us; the launch traced here: 1010 us
  blocking collectives  573 us (56%)
  matrix products  218 us (21%)
  waiting for transfers between devices  132 us (13%)
  other arithmetic  70.4 us (7%)
  between operations  15 us (1%)
    psum x3, blocking collectives, column_step(): lax.psum(partial_value.astype(jnp.bfloat16), 'rows').astype(jnp.float32)  464 us
    reduce_scatter x1, waiting for transfers between devices, local(): lax.psum_scatter(jnp.einsum('rk,rd->kd', piece, student, preferred_elemen...  132 us
    dot_general x3, matrix products, row_step(): partial_value = jnp.dot(expo, col_scale, precision=lax.Precision.HIGHEST)  95.6 us
    psum x1, blocking collectives, local(): mask_total = lax.psum(local_count, 'rows')  78.1 us
    dot_general x3, matrix products, column_step(): partial_value = jnp.dot(weights, expo, precision=lax.Precision.HIGHEST)  60.1 us
    convert_element_type x1, other arithmetic, local(): (row_keep[:, None] * (proto_total * (probs - plan))).astype(jnp.bfloat16)  28.3 us
    mul x1, other arithmetic, local(): expo = row_keep[:, None] * jnp.exp(teach_logit - teach_max[:, None])  24.1 us
    psum x3, blocking collectives, row_step(): rowsum = lax.psum(partial_value, 'protos')  21.7 us
  transfers between devices with their start and end apart: 2, of which 1 were waited for; matrix products, arithmetic and copies ran while one was open for 2% of the time, Pallas kernels for 0%

commit v1 on v0

v1 whole, which is shorter than its diff:
```python
import functools
import math

import jax
import jax.numpy as jnp
from jax import lax
from jax.experimental import pallas as pl
from jax.experimental.pallas import tpu as pltpu
from jax.sharding import Mesh
from jax.sharding import PartitionSpec as P

ITERS = 3
student_temp = 0.1
teacher_temp = 0.05

F32 = jnp.float32
BF16 = jnp.bfloat16
TILE = 256
LANES = 128
FAR = 1e30
INFO = 16
VMEM_LIMIT = 30 * 2**20

NT = (((1,), (1,)), ((), ()))


def params(limit=VMEM_LIMIT):
    return pltpu.CompilerParams(vmem_limit_bytes=limit)


def vmem():
    return pl.BlockSpec(memory_space=pltpu.VMEM)


def smem():
    return pl.BlockSpec(memory_space=pltpu.SMEM)


def split(value):
    high = value.astype(BF16)
    low = (value - high.astype(F32)).astype(BF16)
    return high, low


def as_row(block):
    pieces = []
    for start in range(0, block.shape[0], LANES):
        part = block[start : start + LANES]
        total = part[:, :LANES]
        for lane in range(LANES, block.shape[1], LANES):
            total = total + part[:, lane : lane + LANES]
        pieces.append(jnp.sum(jnp.transpose(total), axis=0, keepdims=True))
    return jnp.concatenate(pieces, axis=1)


def compact_kernel(mask_ref, teach_ref, stud_ref, teach_out, stud_out):
    rows, width = teach_ref.shape
    mask = mask_ref[...]
    down = lax.broadcasted_iota(jnp.int32, (rows, rows), 0)
    along = lax.broadcasted_iota(jnp.int32, (rows, rows), 1)
    upper = jnp.where(down <= along, 1.0, 0.0).astype(BF16)
    many = jnp.broadcast_to(mask, (16, rows)).astype(BF16)
    rank = jnp.dot(many, upper, preferred_element_type=F32)[:1]
    place = jnp.where(mask > 0, rank - 1.0, -1.0)
    onehot = jnp.where(down.astype(F32) == place, 1.0, 0.0).astype(BF16)
    teach_out[:rows] = jnp.dot(onehot, teach_ref[...], preferred_element_type=F32).astype(BF16)
    stud_out[...] = jnp.dot(onehot, stud_ref[...], preferred_element_type=F32).astype(BF16)
    which = lax.broadcasted_iota(jnp.int32, (INFO, width), 0)
    info = jnp.zeros((INFO, width), F32)
    for piece in range(rows // width):
        info = jnp.where(which == piece, mask[:, piece * width : (piece + 1) * width], info)
    teach_out[rows:] = info.astype(BF16)


def compact(mask_row, teacher, student):
    rows, width = teacher.shape
    return pl.pallas_call(
        compact_kernel,
        out_shape=(
            jax.ShapeDtypeStruct((rows + INFO, width), BF16),
            jax.ShapeDtypeStruct((rows, width), BF16),
        ),
        in_specs=[vmem()] * 3,
        out_specs=(vmem(), vmem()),
        compiler_params=params(),
        name="compact",
    )(mask_row, teacher, student)


def max_kernel(teach_ref, proto_ref, out_ref):
    step = pl.program_id(0)
    rows = out_ref.shape[1]
    chunk = 512

    @pl.when(step == 0)
    def _():
        out_ref[...] = jnp.full_like(out_ref, -FAR)

    feats = teach_ref[:rows]
    best = out_ref[...]
    for start in range(0, proto_ref.shape[0], chunk):
        logit = lax.dot_general(
            proto_ref[start : start + chunk], feats, NT, preferred_element_type=F32
        )
        best = jnp.maximum(best, jnp.max(logit, axis=0, keepdims=True))
    out_ref[...] = best


def row_max(feats, protos, rows):
    count, width = protos.shape
    block = 2048
    return pl.pallas_call(
        max_kernel,
        grid=(count // block,),
        out_shape=jax.ShapeDtypeStruct((1, rows), F32),
        in_specs=[
            pl.BlockSpec(feats.shape, lambda i: (0, 0)),
            pl.BlockSpec((block, width), lambda i: (i, 0)),
        ],
        out_specs=pl.BlockSpec((1, rows), lambda i: (0, 0)),
        compiler_params=params(),
        cost_estimate=pl.CostEstimate(
            flops=2 * count * width * rows, bytes_accessed=count * width * 2, transcendentals=0
        ),
        name="row_max",
    )(feats, protos)


def soft_kernel(feat_ref, proto_ref, top_ref, sum_ref):
    step = pl.program_id(0)
    chunk = 512

    @pl.when(step == 0)
    def _():
        top_ref[...] = jnp.full_like(top_ref, -FAR)
        sum_ref[...] = jnp.zeros_like(sum_ref)

    feats = feat_ref[...]
    top = top_ref[...]
    total = sum_ref[...]
    for start in range(0, proto_ref.shape[0], chunk):
        logit = lax.dot_general(
            proto_ref[start : start + chunk], feats, NT, preferred_element_type=F32
        )
        higher = jnp.maximum(top, jnp.max(logit, axis=0, keepdims=True))
        total = total * jnp.exp((top - higher) * (1 / student_temp)) + jnp.sum(
            jnp.exp((logit - higher) * (1 / student_temp)), axis=0, keepdims=True
        )
        top = higher
    top_ref[...] = top
    sum_ref[...] = total


def row_soft(feats, protos):
    count, width = protos.shape
    rows = feats.shape[0]
    block = 2048
    row = pl.BlockSpec((1, rows), lambda i: (0, 0))
    return pl.pallas_call(
        soft_kernel,
        grid=(count // block,),
        out_shape=(jax.ShapeDtypeStruct((1, rows), F32),) * 2,
        in_specs=[
            pl.BlockSpec(feats.shape, lambda i: (0, 0)),
            pl.BlockSpec((block, width), lambda i: (i, 0)),
        ],
        out_specs=(row, row),
        compiler_params=params(),
        cost_estimate=pl.CostEstimate(
            flops=2 * count * width * rows,
            bytes_accessed=count * width * 2,
            transcendentals=count * rows,
        ),
        name="row_soft",
    )(feats, protos)


def load_rows(meta, mine_ref, other_ref, rows_ref, rows):
    blocks = mine_ref.shape[0]
    first = meta[2 * blocks + 2] == 0
    for block in range(blocks):
        offset = pl.multiple_of(meta[block], LANES)
        mine = mine_ref[block, :rows]
        other = other_ref[block, :rows]
        rows_ref[pl.ds(offset, rows), :LANES] = jnp.where(first, mine, other)
        rows_ref[pl.ds(offset, rows), LANES:] = jnp.where(first, other, mine)
    tail = pl.multiple_of(meta[2 * blocks], LANES)
    rows_ref[pl.ds(tail, TILE), :] = jnp.zeros((TILE, rows_ref.shape[1]), BF16)


def load_line(meta, line_ref, out_ref, fill):
    blocks, _, rows = line_ref.shape
    out_ref[...] = jnp.full_like(out_ref, fill)
    lane = lax.broadcasted_iota(jnp.int32, (1, rows), 1)
    for block in range(blocks):
        offset = pl.multiple_of(meta[block], LANES)
        out_ref[:, pl.ds(offset, rows)] = jnp.where(
            lane < meta[blocks + block], line_ref[block], fill
        )


def expo_kernel(meta, mine_ref, other_ref, top_ref, proto_ref, expo_ref, col_ref, valid_ref, rows_ref, line_ref, acc_ref):
    blocks, _, rows = top_ref.shape
    load_rows(meta, mine_ref, other_ref, rows_ref, rows)
    load_line(meta, top_ref, line_ref, FAR)
    valid_ref[...] = jnp.where(line_ref[...] < 0.5 * FAR, 1.0, 0.0)
    acc_ref[...] = jnp.zeros_like(acc_ref)
    chunk = 512

    @pl.loop(0, meta[2 * blocks + 1])
    def _(tile):
        start = pl.multiple_of(tile * TILE, TILE)
        feats = rows_ref[pl.ds(start, TILE), :]
        top = line_ref[:, pl.ds(start, TILE)]
        for k in range(0, proto_ref.shape[0], chunk):
            logit = lax.dot_general(proto_ref[k : k + chunk], feats, NT, preferred_element_type=F32)
            expo = jnp.exp((logit - top) * (1 / teacher_temp))
            expo_ref[tile, k : k + chunk] = expo.astype(BF16)
            acc_ref[k : k + chunk] += expo

    protos = proto_ref.shape[0]
    col_ref[:, :protos] = as_row(acc_ref[...])
    col_ref[:, protos:] = jnp.zeros((1, LANES), F32) + jnp.sum(valid_ref[...])


def expo_step(meta, mine, other, tops, protos):
    blocks, _, rows = tops.shape
    count, width = protos.shape
    total = blocks * rows
    return pl.pallas_call(
        expo_kernel,
        out_shape=(
            pltpu.VMEM((total // TILE, count, TILE), BF16),
            jax.ShapeDtypeStruct((1, count + LANES), F32),
            jax.ShapeDtypeStruct((1, total), F32),
        ),
        in_specs=[smem()] + [vmem()] * 4,
        out_specs=(vmem(),) * 3,
        scratch_shapes=[
            pltpu.VMEM((total + TILE, width), BF16),
            pltpu.VMEM((1, total), F32),
            pltpu.VMEM((count, TILE), F32),
        ],
        compiler_params=params(),
        name="expo",
    )(meta, mine, other, tops, protos)


def col_scale_of(parts_ref, count, proto_total):
    total = parts_ref[0][:, :count]
    for part in range(1, parts_ref.shape[0]):
        total = total + parts_ref[part][:, :count]
    return 1.0 / (proto_total * total)


def row_kernel(proto_total, meta, parts_ref, expo_ref, out_ref):
    count = expo_ref.shape[1]
    high, low = split(col_scale_of(parts_ref, count, proto_total))
    which = lax.broadcasted_iota(jnp.int32, (16, count), 0)
    lhs = jnp.where(which == 0, high.astype(F32), jnp.where(which == 1, low.astype(F32), 0.0)).astype(BF16)
    out_ref[...] = jnp.zeros_like(out_ref)

    @pl.loop(0, meta[17])
    def _(tile):
        start = pl.multiple_of(tile * TILE, TILE)
        both = jnp.dot(lhs, expo_ref[tile], preferred_element_type=F32)
        out_ref[:, pl.ds(start, TILE)] = both[:1] + both[1:2]


def row_step(meta, parts, expo, proto_total):
    tiles, count, _ = expo.shape
    return pl.pallas_call(
        functools.partial(row_kernel, proto_total),
        out_shape=jax.ShapeDtypeStruct((1, tiles * TILE), F32),
        in_specs=[smem()] + [vmem()] * 2,
        out_specs=vmem(),
        compiler_params=params(),
        name="row_step",
    )(meta, parts, expo)


def weights_of(parts_ref, valid_ref):
    total = parts_ref[0]
    for part in range(1, parts_ref.shape[0]):
        total = total + parts_ref[part]
    valid = valid_ref[...]
    return valid / jnp.where(valid > 0, total, 1.0)


def col_kernel(meta, parts_ref, valid_ref, expo_ref, out_ref, line_ref, acc_ref):
    line_ref[...] = weights_of(parts_ref, valid_ref)
    acc_ref[...] = jnp.zeros_like(acc_ref)
    which = lax.broadcasted_iota(jnp.int32, (16, TILE), 0)

    @pl.loop(0, meta[17])
    def _(tile):
        start = pl.multiple_of(tile * TILE, TILE)
        high, low = split(line_ref[:, pl.ds(start, TILE)])
        lhs = jnp.where(which == 0, high.astype(F32), jnp.where(which == 1, low.astype(F32), 0.0)).astype(BF16)
        acc_ref[...] += lax.dot_general(lhs, expo_ref[tile], NT, preferred_element_type=F32)

    out_ref[...] = acc_ref[:1] + acc_ref[1:2]


def col_step(meta, parts, valid, expo):
    tiles, count, _ = expo.shape
    return pl.pallas_call(
        col_kernel,
        out_shape=jax.ShapeDtypeStruct((1, count), F32),
        in_specs=[smem()] + [vmem()] * 3,
        out_specs=vmem(),
        scratch_shapes=[pltpu.VMEM((1, tiles * TILE), F32), pltpu.VMEM((16, count), F32)],
        compiler_params=params(),
        name="col_step",
    )(meta, parts, valid, expo)


def store_blocks(meta, rows_ref, out_ref):
    blocks, rows, _ = out_ref.shape
    for block in range(blocks):
        offset = pl.multiple_of(meta[block], LANES)
        out_ref[block] = rows_ref[pl.ds(offset, rows), :]


def student_kernel(meta, mine_ref, other_ref, lse_ref, proto_ref, turned_ref, grad_ref, feat_ref, rows_ref, line_ref, acc_ref, sums_ref):
    blocks, _, rows = lse_ref.shape
    load_rows(meta, mine_ref, other_ref, rows_ref, rows)
    load_line(meta, lse_ref, line_ref, FAR)
    acc_ref[...] = jnp.zeros_like(acc_ref)
    sums_ref[...] = jnp.zeros_like(sums_ref)
    chunk = 512

    @pl.loop(0, meta[2 * blocks + 1])
    def _(tile):
        start = pl.multiple_of(tile * TILE, TILE)
        feats = rows_ref[pl.ds(start, TILE), :]
        lse = line_ref[:, pl.ds(start, TILE)]
        turned = jnp.zeros((proto_ref.shape[1], TILE), F32)
        for k in range(0, proto_ref.shape[0], chunk):
            logit = lax.dot_general(proto_ref[k : k + chunk], feats, NT, preferred_element_type=F32)
            probs = jnp.exp(logit * (1 / student_temp) - lse).astype(BF16)
            acc_ref[k : k + chunk] += jnp.dot(probs, feats, preferred_element_type=F32)
            turned += jnp.dot(turned_ref[:, k : k + chunk], probs, preferred_element_type=F32)
        sums_ref[pl.ds(start, TILE), :] = jnp.transpose(turned).astype(BF16)

    store_blocks(meta, sums_ref, feat_ref)
    grad_ref[...] = acc_ref[...].astype(BF16)


def student_step(meta, mine, other, lses, protos, turned):
    blocks, _, rows = lses.shape
    count, width = protos.shape
    total = blocks * rows
    return pl.pallas_call(
        student_kernel,
        out_shape=(
            jax.ShapeDtypeStruct((count, width), BF16),
            jax.ShapeDtypeStruct((blocks, rows, width), BF16),
        ),
        in_specs=[smem()] + [vmem()] * 5,
        out_specs=(vmem(),) * 2,
        scratch_shapes=[
            pltpu.VMEM((total + TILE, width), BF16),
            pltpu.VMEM((1, total), F32),
            pltpu.VMEM((count, width), F32),
            pltpu.VMEM((total, width), BF16),
        ],
        compiler_params=params(),
        name="student",
    )(meta, mine, other, lses, protos, turned)


def feature_kernel(proto_total, meta, parts_ref, expo_ref, turned_ref, feat_ref, sums_ref):
    count = expo_ref.shape[1]
    scale = col_scale_of(parts_ref, count, proto_total)
    scaled = (turned_ref[...].astype(F32) * scale).astype(BF16)
    sums_ref[...] = jnp.zeros_like(sums_ref)

    @pl.loop(0, meta[17])
    def _(tile):
        start = pl.multiple_of(tile * TILE, TILE)
        turned = jnp.dot(scaled, expo_ref[tile], preferred_element_type=F32)
        sums_ref[pl.ds(start, TILE), :] = jnp.transpose(turned).astype(BF16)

    store_blocks(meta, sums_ref, feat_ref)


def feature_step(meta, parts, expo, turned, proto_total):
    tiles, count, _ = expo.shape
    width = turned.shape[0]
    return pl.pallas_call(
        functools.partial(feature_kernel, proto_total),
        out_shape=jax.ShapeDtypeStruct((8, tiles * TILE // 8, width), BF16),
        in_specs=[smem()] + [vmem()] * 3,
        out_specs=vmem(),
        scratch_shapes=[pltpu.VMEM((tiles * TILE, width), BF16)],
        compiler_params=params(),
        name="feature_step",
    )(meta, parts, expo, turned)


def grad_kernel(meta, parts_ref, valid_ref, mine_ref, other_ref, expo_ref, grad_ref, weight_ref, rows_ref, acc_ref):
    blocks = mine_ref.shape[0]
    load_rows(meta, mine_ref, other_ref, rows_ref, mine_ref.shape[1])
    weight_ref[...] = weights_of(parts_ref, valid_ref)
    acc_ref[...] = jnp.zeros_like(acc_ref)
    chunk = 512

    @pl.loop(0, meta[2 * blocks + 1])
    def _(tile):
        start = pl.multiple_of(tile * TILE, TILE)
        weight = weight_ref[:, pl.ds(start, TILE)]
        feats = rows_ref[pl.ds(start, TILE), :].astype(F32)
        parts = []
        for lane in range(0, TILE, LANES):
            column = jnp.transpose(jnp.broadcast_to(weight[:, lane : lane + LANES], (LANES, LANES)))
            part = feats[lane : lane + LANES]
            parts.append(
                jnp.concatenate(
                    [part[:, d : d + LANES] * column for d in range(0, part.shape[1], LANES)], axis=1
                )
            )
        scaled = jnp.concatenate(parts, axis=0).astype(BF16)
        for k in range(0, acc_ref.shape[0], chunk):
            acc_ref[k : k + chunk] += jnp.dot(
                expo_ref[tile, k : k + chunk], scaled, preferred_element_type=F32
            )

    grad_ref[...] = acc_ref[...].astype(BF16)


def grad_step(meta, parts, valid, mine, other, expo):
    tiles, count, _ = expo.shape
    width = 2 * LANES
    total = tiles * TILE
    return pl.pallas_call(
        grad_kernel,
        out_shape=(
            jax.ShapeDtypeStruct((count, width), BF16),
            jax.ShapeDtypeStruct((1, total), F32),
        ),
        in_specs=[smem()] + [vmem()] * 5,
        out_specs=(vmem(),) * 2,
        scratch_shapes=[
            pltpu.VMEM((total + TILE, width), BF16),
            pltpu.VMEM((count, width), F32),
        ],
        compiler_params=params(),
        name="grad_step",
    )(meta, parts, valid, mine, other, expo)


def swap(value, axis):
    return lax.ppermute(value, axis, [(0, 1), (1, 0)])


def spread(value, axes, size):
    many = jnp.broadcast_to(value[None], (size,) + value.shape)
    return lax.all_to_all(many, axes, 0, 0, tiled=True)


def gather_blocks(block, core):
    half = lax.dynamic_slice_in_dim(block, core * LANES, LANES, 1)
    beside = swap(half, "xl")
    low = lax.axis_index("xl") == 0
    pair = jnp.stack([jnp.where(low, half, beside), jnp.where(low, beside, half)])
    mine = spread(pair, "y", 4)
    mine = mine.reshape((8,) + half.shape)
    return mine, swap(mine, "c")


def scatter_rows(value, core):
    blocks, rows, width = value.shape
    width //= 2
    value = value.reshape(blocks * rows, 2 * width)
    keep = lax.dynamic_slice_in_dim(value, core * width, width, 1)
    give = lax.dynamic_slice_in_dim(value, (1 - core) * width, width, 1)
    total = (keep.astype(F32) + swap(give, "c").astype(F32)).astype(BF16)
    parts = lax.all_to_all(total.reshape(4, -1, width), "y", 0, 0, tiled=True)
    total = jnp.sum(parts.astype(F32), axis=0).astype(BF16)
    rows = total.shape[0] // 2
    side = lax.axis_index("xl")
    keep = lax.dynamic_slice_in_dim(total, side * rows, rows, 0)
    give = lax.dynamic_slice_in_dim(total, (1 - side) * rows, rows, 0)
    return keep.astype(F32) + swap(give, "xl").astype(F32)


def local(student, teacher, prototypes, masked):
    rows, width = student.shape
    y, xl, z = lax.axis_index("y"), lax.axis_index("xl"), lax.axis_index("z")
    xh, core = lax.axis_index("xh"), lax.axis_index("c")
    block_id = y * 2 + xl
    count = prototypes.shape[0] // 8
    proto_total = prototypes.shape[0] * 4
    mask_row = masked.astype(F32)[None]

    teach, stud = compact(mask_row, teacher, student)
    protos = lax.dynamic_slice_in_dim(prototypes, block_id * count, count, 0)
    turned = jnp.transpose(protos)

    mine, other = gather_blocks(teach, core)
    top = row_max(teach, prototypes, rows)
    top = jnp.maximum(top, swap(top, "c"))
    top = jnp.maximum(top, swap(top, "xh"))
    tops = spread(top, ("y", "xl"), 8)

    counts = jnp.sum(mine[:, rows:].astype(F32), axis=(1, 2)) + jnp.sum(other[:, rows:].astype(F32), axis=(1, 2))
    counts = counts.astype(jnp.int32)
    padded = (counts + (LANES - 1)) // LANES * LANES
    ends = jnp.cumsum(padded)
    tail = ends[-1:]
    meta = jnp.concatenate(
        [ends - padded, counts, tail, (tail + (TILE - 1)) // TILE, core.astype(jnp.int32)[None]]
    )

    expo, col, valid = expo_step(meta, mine, other, tops, protos)
    col_parts = spread(col, "z", 4)
    mask_total = jnp.sum(col_parts[:, 0, count])

    stud_mine, stud_other = gather_blocks(stud, core)
    soft_top, soft_sum = row_soft(stud, prototypes)
    for axis in ("c", "xh"):
        far_top, far_sum = swap(soft_top, axis), swap(soft_sum, axis)
        high = jnp.maximum(soft_top, far_top)
        soft_sum = soft_sum * jnp.exp((soft_top - high) / student_temp) + far_sum * jnp.exp(
            (far_top - high) / student_temp
        )
        soft_top = high
    lse = soft_top / student_temp + jnp.log(soft_sum)
    lses = spread(lse, ("y", "xl"), 8)
    stud_grad, stud_feat = student_step(meta, stud_mine, stud_other, lses, protos, turned)

    for iteration in range(ITERS):
        row = row_step(meta, col_parts, expo, proto_total)
        row = row + swap(row, "c")
        row_parts = spread(row, ("y", "xl", "xh"), 16)
        if iteration < ITERS - 1:
            col = col_step(meta, row_parts, valid, expo)
            col_parts = spread(col, "z", 4)

    plan_feat = feature_step(meta, col_parts, expo, turned, proto_total)
    plan_own = scatter_rows(plan_feat, core)
    stud_own = scatter_rows(stud_feat, core)

    plan_grad, weights = grad_step(meta, row_parts, valid, stud_mine, stud_other, expo)

    half = width // 2
    weight_row = lax.dynamic_slice(weights, (0, meta[block_id]), (1, rows))
    own = (stud_own - weight_row[0][:, None] * plan_own).astype(BF16)
    place = jnp.where(masked > 0, jnp.cumsum(masked) - 1, -1)
    onehot = (place[:, None] == jnp.arange(rows)[None, :]).astype(BF16)
    own = jnp.dot(onehot, own, preferred_element_type=F32)
    keep = lax.dynamic_slice_in_dim(own, xh * (rows // 2), rows // 2, 0)
    give = lax.dynamic_slice_in_dim(own, (1 - xh) * (rows // 2), rows // 2, 0)
    own = keep + swap(give.astype(BF16), "xh").astype(F32)
    quarter = rows // 4
    keep = lax.dynamic_slice_in_dim(own, core * quarter, quarter, 0)
    give = lax.dynamic_slice_in_dim(own, (1 - core) * quarter, quarter, 0)
    got = swap(give.astype(BF16), "c").astype(F32)
    joined = jnp.where(core == 0, jnp.concatenate([keep, got], 1), jnp.concatenate([got, keep], 1))
    feature_grad = (joined * (math.sqrt(proto_total) / student_temp)).astype(BF16)

    stud_parts = lax.all_to_all(stud_grad.reshape(4, -1, width), "z", 0, 0, tiled=True)
    plan_parts = lax.all_to_all(plan_grad.reshape(4, -1, width), "z", 0, 0, tiled=True)
    col_total = jnp.sum(col_parts[:, 0, :count], axis=0)
    scale = 1.0 / (proto_total * lax.dynamic_slice_in_dim(col_total, z * (count // 4), count // 4, 0))
    stud_sum = jnp.sum(stud_parts.astype(F32), axis=0)
    plan_sum = jnp.sum(plan_parts.astype(F32), axis=0)
    proto_grad = (
        (stud_sum - scale[:, None] * plan_sum) * (proto_total / jnp.sqrt(mask_total))
    ).astype(BF16)
    return feature_grad, proto_grad


def solution(mesh):
    fine = Mesh(mesh.devices.reshape(4, 2, 4, 2, 2), ("y", "xl", "z", "xh", "c"))
    rows, protos = ("y", "xl", "z"), ("xh", "c")
    in_specs = (P(rows, None), P(rows, None), P(protos, None), P(rows))
    out_specs = (P(rows + protos, None), P(protos + rows, None))
    return jax.shard_map(local, mesh=fine, in_specs=in_specs, out_specs=out_specs, check_vma=False)
```

time: 1020 us -> 322 us (0.32)
  blocking collectives: 573 us -> 21.5 us
  matrix products: 218 us -> 0.52 us
  Pallas kernels: 0 us -> 77.1 us
  starting transfers between devices: 0.08 us -> 69.4 us
  waiting for transfers between devices: 132 us -> 63.6 us
  local copies, waits for them, and re-layouts: 0.89 us -> 68 us
  other arithmetic: 70.4 us -> 13.8 us
  between operations: 15 us -> 4.46 us
    psum x7 -> x0, blocking collectives: 563 us -> none  [the longest x3 464 us: column_step(): lax.psum(partial_value.astype(jnp.bfloat16), 'rows').astype(jnp.float32)]
    dot_general x10 -> x1, matrix products: 218 us -> 0.52 us  [local(): own = jnp.dot(onehot, own, preferred_element_type=F32)]
    reduce_scatter x2 -> x0, waiting for transfers between devices: 132 us -> none  [the longest x1 132 us: local(): lax.psum_scatter(jnp.einsum('rk,rd->kd', piece, student, preferred_elemen...]
    pallas_call x0 -> x12, Pallas kernels: none -> 77.1 us  [the longest x1 16.5 us: student_step(): pl.pallas_call(student_kernel, out_shape=(jax.ShapeDtypeStruct((count, wi...]
    unnamed x6 -> x36, local copies, waits for them, and re-layouts: 0.89 us -> 54 us
    all_to_all x0 -> x12, starting transfers between devices: none -> 53.1 us  [the longest x8 35.6 us: spread(): return lax.all_to_all(many, axes, 0, 0, tiled=True)]
    all_to_all x0 -> x12, waiting for transfers between devices: none -> 52.8 us  [the longest x8 35.6 us: spread(): return lax.all_to_all(many, axes, 0, 0, tiled=True)]
    convert_element_type x7 -> x6, other arithmetic: 31.6 us -> 7.17 us  [the longest x2 5.46 us: scatter_rows(): total = (keep.astype(F32) + swap(give, 'c').astype(F32)).astype(BF16)]
  transfers between devices with their start and end apart: 2 -> 31, of which waited for: 1 -> 15; matrix products, arithmetic and copies ran while one was open for 2% -> 8% of each run, Pallas kernels for 0% -> 24%
where the time goes in v1:
time: 322 us; the launch traced here: 318 us
  Pallas kernels  77.1 us (24%)
  starting transfers between devices  69.4 us (22%)
  local copies, waits for them, and re-layouts  68 us (21%)
  waiting for transfers between devices  63.6 us (20%)
  blocking collectives  21.5 us (7%)
  other arithmetic  13.8 us (4%)
  between operations  4.46 us (1%)
    unnamed x36, local copies, waits for them, and re-layouts  54 us
    all_to_all x8, waiting for transfers between devices, spread(): return lax.all_to_all(many, axes, 0, 0, tiled=True)  35.6 us
    all_to_all x8, starting transfers between devices, spread(): return lax.all_to_all(many, axes, 0, 0, tiled=True)  35.6 us
    all_to_all x2, blocking collectives, spread(): return lax.all_to_all(many, axes, 0, 0, tiled=True)  21.5 us
    pallas_call x1, Pallas kernels, student_step(): pl.pallas_call(student_kernel, out_shape=(jax.ShapeDtypeStruct((count, wi...  16.5 us
    ppermute x19, starting transfers between devices, swap(): return lax.ppermute(value, axis, [(0, 1), (1, 0)])  16.3 us
    pallas_call x1, Pallas kernels, row_soft(): pl.pallas_call(soft_kernel, grid=(count // block,), out_shape=(jax.ShapeD...  12.9 us
    all_to_all x2, waiting for transfers between devices, scatter_rows(): parts = lax.all_to_all(total.reshape(4, -1, width), 'y', 0, 0, tiled=True)  12 us
  transfers between devices with their start and end apart: 31, of which 15 were waited for; matrix products, arithmetic and copies ran while one was open for 8% of the time, Pallas kernels for 24%

profile of v1, /device:TPU:0, one launch (start us, length us, event | category | flops | bytes accessed | tf_op | source)
XLA Modules:
  0.0 318.4 jit_solution(16923198469555642495)
XLA Ops:
  6.9 3.6 %collective-permute-done = bf16[528,128]{1,0:T(8,128)(2,1)S(1)} collective-permute-done((bf16[528,128]{1,0:T(8,128)(2,1)S(1)}, bf16[528,128]{1,0:T(8,128)(2,1)S(1)}, u32[]{:S(2)}, u32[]{:S(2)}) %collective-permute-start) | collective-permute-done | bytes 135200 | tf_op jit(solution)/shard_map/ppermute | solution.py:454
  11.7 4.7 %all-to-all-start = ((bf16[4,2,528,128]{3,2,1,0:T(8,128)(2,1)}), bf16[4,2,528,128]{3,2,1,0:T(8,128)(2,1)S(1)}, u32[]{:S(2)}, u32[]{:S(2)}) async-start(bf16[4,2,528,128]{3,2,1,0:T(8,128)(2,1)} %broadcast_in_dim.42), calls=%async_computation | async-start | bytes 2162688 | tf_op jit(solution)/shard_map/all_to_all | solution.py:459
  18.0 13.0 %all-to-all-done = bf16[4,2,528,128]{3,2,1,0:T(8,128)(2,1)S(1)} async-done(((bf16[4,2,528,128]{3,2,1,0:T(8,128)(2,1)}), bf16[4,2,528,128]{3,2,1,0:T(8,128)(2,1)S(1)}, u32[]{:S(2)}, u32[]{:S(2)}) %all-to-all-start) | async-done | bytes 1081376 | tf_op jit(solution)/shard_map/all_to_all | solution.py:459
  39.1 6.1 %row_max.1 = f32[1,512]{1,0:T(1,128)S(1)} custom-call(bf16[528,256]{1,0:T(8,128)(2,1)S(1)} %get-tuple-element.13.teach_ref, bf16[16384,256]{1,0:T(8,128)(2,1)S(1)} %copy-done.13), custom_call_target="tpu_custom_call" | custom-call | flops 4294967296 | bytes 8388608 | tf_op jit(solution)/shard_map/row_max/pallas_call | solution.py:112
  52.4 5.5 %all-to-all-start.4 = ((f32[8,1,512]{2,1,0:T(1,128)}), f32[8,1,512]{2,1,0:T(1,128)S(1)}, u32[]{:S(2)}, u32[]{:S(2)}) async-start(f32[8,1,512]{2,1,0:T(1,128)} %broadcast_in_dim.94), calls=%async_computation.4 | async-start | bytes 32768 | tf_op jit(solution)/shard_map/all_to_all | solution.py:459
  64.1 8.5 %expo.1 = (bf16[16,2048,256]{2,1,0:T(8,128)(2,1)S(1)}, f32[1,2176]{1,0:T(1,128)S(1)}, f32[1,4096]{1,0:T(1,128)S(1)}) custom-call(s32[19]{0:T(128)S(1)} %concatenate.9.meta, bf16[8,528,128]{2,1,0:T(8,128)(2,1)S(1)} %bitcast.53, bf16[8,528,128]{2,1,0:T(8,128)(2,1)} %collective-permute-done.1.other_ref, f32[8,1,512]{2,1,0:T(1,128)S(1)} %all-to-all-done.4.top_ref, ...), custom_call_target="tpu_custom_call" | custom-call | tf_op jit(solution)/shard_map/expo/pallas_call | solution.py:230
  72.6 5.7 %copy-done = bf16[16,2048,256]{2,1,0:T(8,128)(2,1)} copy-done((bf16[16,2048,256]{2,1,0:T(8,128)(2,1)}, bf16[16,2048,256]{2,1,0:T(8,128)(2,1)S(1)}, u32[]{:S(2)}) %copy-start) | copy-done | bytes 16777240
  78.4 11.2 %all_to_all.70.parts_ref = f32[4,1,2176]{2,1,0:T(1,128)S(1)} all-to-all(f32[4,1,2176]{2,1,0:T(1,128)S(1)} %broadcast_in_dim.96), channel_id=1, replica_groups=mesh['y'=4,'xl'=2,'z'=4,'xh'=2,'c'=2] {'z'}, dimensions={0} | all-to-all | bytes 69632 | tf_op jit(solution)/shard_map/all_to_all | solution.py:459
  89.6 5.8 %copy-done.1 = bf16[16,2048,256]{2,1,0:T(8,128)(2,1)S(1)} copy-done((bf16[16,2048,256]{2,1,0:T(8,128)(2,1)S(1)}, bf16[16,2048,256]{2,1,0:T(8,128)(2,1)}, u32[]{:S(2)}) %copy-start.1) | copy-done | bytes 16777240
  100.6 4.7 %all-to-all-start.6 = ((f32[16,1,4096]{2,1,0:T(1,128)}), f32[16,1,4096]{2,1,0:T(1,128)S(1)}, u32[]{:S(2)}, u32[]{:S(2)}) async-start(f32[16,1,4096]{2,1,0:T(1,128)} %broadcast_in_dim.98), calls=%async_computation.6 | async-start | bytes 524288 | tf_op jit(solution)/shard_map/all_to_all | solution.py:459
  108.7 12.9 %row_soft.1 = (f32[1,512]{1,0:T(1,128)S(1)}, f32[1,512]{1,0:T(1,128)S(1)}) custom-call(bf16[512,256]{1,0:T(8,128)(2,1)S(1)} %get-tuple-element.14.feat_ref, bf16[16384,256]{1,0:T(8,128)(2,1)S(1)} %copy-done.14), custom_call_target="tpu_custom_call" | custom-call | flops 4294967296 | bytes 8388608 | tf_op jit(solution)/shard_map/row_soft/pallas_call | solution.py:159
  122.2 5.8 %copy-done.2 = bf16[16,2048,256]{2,1,0:T(8,128)(2,1)S(1)} copy-done((bf16[16,2048,256]{2,1,0:T(8,128)(2,1)S(1)}, bf16[16,2048,256]{2,1,0:T(8,128)(2,1)}, u32[]{:S(2)}) %copy-start.2) | copy-done | bytes 16777240
  128.0 4.5 %col_step.2 = f32[1,2048]{1,0:T(1,128)S(1)} custom-call(s32[19]{0:T(128)S(1)} %concatenate.9.meta, f32[16,1,4096]{2,1,0:T(1,128)S(1)} %all-to-all-done.6.parts_ref, f32[1,4096]{1,0:T(1,128)S(1)} %get-tuple-element.20.valid_ref, bf16[16,2048,256]{2,1,0:T(8,128)(2,1)S(1)} %copy-done.2), custom_call_target="tpu_custom_call" | custom-call | tf_op jit(solution)/shard_map/col_step/pallas_call | solution.py:307
  141.8 5.8 %copy-done.3 = bf16[16,2048,256]{2,1,0:T(8,128)(2,1)S(1)} copy-done((bf16[16,2048,256]{2,1,0:T(8,128)(2,1)S(1)}, bf16[16,2048,256]{2,1,0:T(8,128)(2,1)}, u32[]{:S(2)}) %copy-start.3) | copy-done | bytes 16777240
  151.4 5.6 %all-to-all-start.2 = ((f32[8,1,512]{2,1,0:T(1,128)}), f32[8,1,512]{2,1,0:T(1,128)S(1)}, u32[]{:S(2)}, u32[]{:S(2)}) async-start(f32[8,1,512]{2,1,0:T(1,128)} %broadcast_in_dim.92), calls=%async_computation.2 | async-start | bytes 32768 | tf_op jit(solution)/shard_map/all_to_all | solution.py:459
  157.6 5.6 %all-to-all-done.2.lse_ref = f32[8,1,512]{2,1,0:T(1,128)S(1)} async-done(((f32[8,1,512]{2,1,0:T(1,128)}), f32[8,1,512]{2,1,0:T(1,128)S(1)}, u32[]{:S(2)}, u32[]{:S(2)}) %all-to-all-start.2) | async-done | bytes 16416 | tf_op jit(solution)/shard_map/all_to_all | solution.py:459
  163.2 16.5 %student.1 = (bf16[2048,256]{1,0:T(8,128)(2,1)S(1)}, bf16[8,512,256]{2,1,0:T(8,128)(2,1)S(1)}) custom-call(s32[19]{0:T(128)S(1)} %concatenate.9.meta, bf16[8,512,128]{2,1,0:T(8,128)(2,1)S(1)} %bitcast.45, bf16[8,512,128]{2,1,0:T(8,128)(2,1)} %collective-permute-done.3.other_ref, f32[8,1,512]{2,1,0:T(1,128)S(1)} %all-to-all-done.2.lse_ref, ...), custom_call_target="tpu_custom_call" | custom-call | tf_op jit(solution)/shard_map/student/pallas_call | solution.py:354
  182.9 4.7 %all-to-all-start.8 = ((f32[16,1,4096]{2,1,0:T(1,128)}), f32[16,1,4096]{2,1,0:T(1,128)S(1)}, u32[]{:S(2)}, u32[]{:S(2)}) async-start(f32[16,1,4096]{2,1,0:T(1,128)} %broadcast_in_dim.102), calls=%async_computation.8 | async-start | bytes 524288 | tf_op jit(solution)/shard_map/all_to_all | solution.py:459
  189.9 6.1 %all-to-all-done.8.parts_ref = f32[16,1,4096]{2,1,0:T(1,128)S(1)} async-done(((f32[16,1,4096]{2,1,0:T(1,128)}), f32[16,1,4096]{2,1,0:T(1,128)S(1)}, u32[]{:S(2)}, u32[]{:S(2)}) %all-to-all-start.8) | async-done | bytes 262176 | tf_op jit(solution)/shard_map/all_to_all | solution.py:459
  196.0 5.8 %copy-done.4 = bf16[16,2048,256]{2,1,0:T(8,128)(2,1)S(1)} copy-done((bf16[16,2048,256]{2,1,0:T(8,128)(2,1)S(1)}, bf16[16,2048,256]{2,1,0:T(8,128)(2,1)}, u32[]{:S(2)}) %copy-start.4) | copy-done | bytes 16777240
  201.8 4.5 %col_step.3 = f32[1,2048]{1,0:T(1,128)S(1)} custom-call(s32[19]{0:T(128)S(1)} %concatenate.9.meta, f32[16,1,4096]{2,1,0:T(1,128)S(1)} %all-to-all-done.8.parts_ref, f32[1,4096]{1,0:T(1,128)S(1)} %get-tuple-element.20.valid_ref, bf16[16,2048,256]{2,1,0:T(8,128)(2,1)S(1)} %copy-done.4), custom_call_target="tpu_custom_call" | custom-call | tf_op jit(solution)/shard_map/col_step/pallas_call | solution.py:307
  206.3 10.3 %all_to_all.71.parts_ref = f32[4,1,2048]{2,1,0:T(1,128)S(1)} all-to-all(f32[4,1,2048]{2,1,0:T(1,128)S(1)} %broadcast_in_dim.104), channel_id=1, replica_groups=mesh['y'=4,'xl'=2,'z'=4,'xh'=2,'c'=2] {'z'}, dimensions={0} | all-to-all | bytes 65536 | tf_op jit(solution)/shard_map/all_to_all | solution.py:459
  220.1 5.8 %copy-done.5 = bf16[16,2048,256]{2,1,0:T(8,128)(2,1)S(1)} copy-done((bf16[16,2048,256]{2,1,0:T(8,128)(2,1)S(1)}, bf16[16,2048,256]{2,1,0:T(8,128)(2,1)}, u32[]{:S(2)}) %copy-start.5) | copy-done | bytes 16777240
  225.9 6.1 %feature_step.1 = bf16[8,512,256]{2,1,0:T(8,128)(2,1)S(1)} custom-call(s32[19]{0:T(128)S(1)} %concatenate.9.meta, f32[4,1,2048]{2,1,0:T(1,128)S(1)} %all_to_all.71.parts_ref, bf16[16,2048,256]{2,1,0:T(8,128)(2,1)S(1)} %copy-done.5, bf16[256,2048]{1,0:T(8,128)(2,1)S(1)} %bitcast.48), custom_call_target="tpu_custom_call" | custom-call | tf_op jit(solution)/shard_map/feature_step/pallas_call | solution.py:391
  240.1 3.5 %all-to-all-start.10 = ((f32[16,1,4096]{2,1,0:T(1,128)}), f32[16,1,4096]{2,1,0:T(1,128)S(1)}, u32[]{:S(2)}, u32[]{:S(2)}) async-start(f32[16,1,4096]{2,1,0:T(1,128)} %broadcast_in_dim.106), calls=%async_computation.10 | async-start | bytes 524288 | tf_op jit(solution)/shard_map/all_to_all | solution.py:459
  246.6 6.2 %all-to-all-done.10.parts_ref = f32[16,1,4096]{2,1,0:T(1,128)S(1)} async-done(((f32[16,1,4096]{2,1,0:T(1,128)}), f32[16,1,4096]{2,1,0:T(1,128)S(1)}, u32[]{:S(2)}, u32[]{:S(2)}) %all-to-all-start.10) | async-done | bytes 262176 | tf_op jit(solution)/shard_map/all_to_all | solution.py:459
  252.8 4.3 %all-to-all-start.3 = ((bf16[4,1024,128]{2,1,0:T(8,128)(2,1)}), bf16[4,1024,128]{2,1,0:T(8,128)(2,1)}, u32[]{:S(2)}, u32[]{:S(2)}) async-start(bf16[4,1024,128]{2,1,0:T(8,128)(2,1)} %bitcast.61), calls=%async_computation.3 | async-start | bytes 2097152 | tf_op jit(solution)/shard_map/all_to_all | solution.py:479
  259.6 12.0 %all-to-all-done.3 = bf16[4,1024,128]{2,1,0:T(8,128)(2,1)} async-done(((bf16[4,1024,128]{2,1,0:T(8,128)(2,1)}), bf16[4,1024,128]{2,1,0:T(8,128)(2,1)}, u32[]{:S(2)}, u32[]{:S(2)}) %all-to-all-start.3) | async-done | bytes 1048608 | tf_op jit(solution)/shard_map/all_to_all | solution.py:479
  275.1 5.8 %copy-done.6 = bf16[16,2048,256]{2,1,0:T(8,128)(2,1)S(1)} copy-done((bf16[16,2048,256]{2,1,0:T(8,128)(2,1)S(1)}, bf16[16,2048,256]{2,1,0:T(8,128)(2,1)}, u32[]{:S(2)}) %copy-start.6) | copy-done | bytes 16777240
  280.9 8.1 %grad_step.1 = (bf16[2048,256]{1,0:T(8,128)(2,1)}, f32[1,4096]{1,0:T(1,128)S(1)}) custom-call(s32[19]{0:T(128)S(1)} %concatenate.9.meta, f32[16,1,4096]{2,1,0:T(1,128)S(1)} %all-to-all-done.10.parts_ref, f32[1,4096]{1,0:T(1,128)S(1)} %get-tuple-element.20.valid_ref, bf16[8,512,128]{2,1,0:T(8,128)(2,1)S(1)} %bitcast.46, ...), custom_call_target="tpu_custom_call" | custom-call | tf_op jit(solution)/shard_map/grad_step/pallas_call | solution.py:436
  288.9 6.2 %all-to-all-start.13 = ((bf16[4,512,256]{2,1,0:T(8,128)(2,1)}), bf16[4,512,256]{2,1,0:T(8,128)(2,1)}, u32[]{:S(2)}, u32[]{:S(2)}) async-start(bf16[4,512,256]{2,1,0:T(8,128)(2,1)} %bitcast.28), calls=%async_computation.13 | async-start | bytes 2097152 | tf_op jit(solution)/shard_map/all_to_all | solution.py:564
  303.3 5.2 %all-to-all-done.13 = bf16[4,512,256]{2,1,0:T(8,128)(2,1)} async-done(((bf16[4,512,256]{2,1,0:T(8,128)(2,1)}), bf16[4,512,256]{2,1,0:T(8,128)(2,1)}, u32[]{:S(2)}, u32[]{:S(2)}) %all-to-all-start.13) | async-done | bytes 1048608 | tf_op jit(solution)/shard_map/all_to_all | solution.py:564
  (140 shorter events, 94.2 us)
Async XLA Ops:
  5.2 5.2 %collective-permute-start = (bf16[528,128]{1,0:T(8,128)(2,1)S(1)}, bf16[528,128]{1,0:T(8,128)(2,1)S(1)}, u32[]{:S(2)}, u32[]{:S(2)}) collective-permute-start(bf16[528,128]{1,0:T(8,128)(2,1)S(1)} %constant_dynamic-slice_fusion.8), channel_id=1, source_target_pairs={{0,16},{16,0},{1,17},{17,1},{2,18},{18,2},{3,19},{19,3},{4,20},{20... | collective-permute-start | bytes 405512 | tf_op jit(solution)/shard_map/ppermute | solution.py:454
  11.7 19.3 %all-to-all-start = ((bf16[4,2,528,128]{3,2,1,0:T(8,128)(2,1)}), bf16[4,2,528,128]{3,2,1,0:T(8,128)(2,1)S(1)}, u32[]{:S(2)}, u32[]{:S(2)}) async-start(bf16[4,2,528,128]{3,2,1,0:T(8,128)(2,1)} %broadcast_in_dim.42), calls=%async_computation | async-start | bytes 2162688 | tf_op jit(solution)/shard_map/all_to_all | solution.py:459
  16.4 14.6 %collective-permute-start.2 = (bf16[512,128]{1,0:T(8,128)(2,1)S(1)}, bf16[512,128]{1,0:T(8,128)(2,1)S(1)}, u32[]{:S(2)}, u32[]{:S(2)}) collective-permute-start(bf16[512,128]{1,0:T(8,128)(2,1)S(1)} %constant_dynamic-slice_fusion.7), channel_id=1, source_target_pairs={{0,16},{16,0},{1,17},{17,1},{2,18},{18,2},{3,19},{19,3},{4,20},{20... | collective-permute-start | bytes 393224 | tf_op jit(solution)/shard_map/ppermute | solution.py:454
  31.0 27.1 %collective-permute-start.1 = (bf16[8,528,128]{2,1,0:T(8,128)(2,1)S(1)}, bf16[8,528,128]{2,1,0:T(8,128)(2,1)}, u32[]{:S(2)}, u32[]{:S(2)}) collective-permute-start(bf16[8,528,128]{2,1,0:T(8,128)(2,1)S(1)} %bitcast.51), channel_id=1, source_target_pairs={{0,1},{1,0},{2,3},{3,2},{4,5},{5,4},{6,7},{7,6},{8,9},{9,8},{10,11... | collective-permute-start | bytes 3244040 | tf_op jit(solution)/shard_map/ppermute | solution.py:454
  32.2 19.6 %all-to-all-start.1 = ((bf16[4,2,512,128]{3,2,1,0:T(8,128)(2,1)}), bf16[4,2,512,128]{3,2,1,0:T(8,128)(2,1)S(1)}, u32[]{:S(2)}, u32[]{:S(2)}) async-start(bf16[4,2,512,128]{3,2,1,0:T(8,128)(2,1)} %broadcast_in_dim.45), calls=%async_computation.1 | async-start | bytes 2097152 | tf_op jit(solution)/shard_map/all_to_all | solution.py:459
  45.2 1.4 collective-permute-start.10
  46.7 5.1 %collective-permute-start.11 = (f32[1,512]{1,0:T(1,128)S(1)}, f32[1,512]{1,0:T(1,128)S(1)}, u32[]{:S(2)}, u32[]{:S(2)}) collective-permute-start(f32[1,512]{1,0:T(1,128)S(1)} %max.14), channel_id=1, source_target_pairs={{0,2},{2,0},{1,3},{3,1},{4,6},{6,4},{5,7},{7,5},{8,10},{10,8},{9,1... | collective-permute-start | bytes 6152 | tf_op jit(solution)/shard_map/ppermute | solution.py:454
  52.4 11.7 %all-to-all-start.4 = ((f32[8,1,512]{2,1,0:T(1,128)}), f32[8,1,512]{2,1,0:T(1,128)S(1)}, u32[]{:S(2)}, u32[]{:S(2)}) async-start(f32[8,1,512]{2,1,0:T(1,128)} %broadcast_in_dim.94), calls=%async_computation.4 | async-start | bytes 32768 | tf_op jit(solution)/shard_map/all_to_all | solution.py:459
  57.9 105.3 %collective-permute-start.3 = (bf16[8,512,128]{2,1,0:T(8,128)(2,1)S(1)}, bf16[8,512,128]{2,1,0:T(8,128)(2,1)}, u32[]{:S(2)}, u32[]{:S(2)}) collective-permute-start(bf16[8,512,128]{2,1,0:T(8,128)(2,1)S(1)} %bitcast.44), channel_id=1, source_target_pairs={{0,1},{1,0},{2,3},{3,2},{4,5},{5,4},{6,7},{7,6},{8,9},{9,8},{10,11... | collective-permute-start | bytes 3145736 | tf_op jit(solution)/shard_map/ppermute | solution.py:454
  98.5 1.2 collective-permute-start.12
  100.6 21.6 %all-to-all-start.6 = ((f32[16,1,4096]{2,1,0:T(1,128)}), f32[16,1,4096]{2,1,0:T(1,128)S(1)}, u32[]{:S(2)}, u32[]{:S(2)}) async-start(f32[16,1,4096]{2,1,0:T(1,128)} %broadcast_in_dim.98), calls=%async_computation.6 | async-start | bytes 524288 | tf_op jit(solution)/shard_map/all_to_all | solution.py:459
  121.6 14.7 %collective-permute-start.4 = (f32[1,512]{1,0:T(1,128)S(1)}, f32[1,512]{1,0:T(1,128)S(1)}, u32[]{:S(2)}, u32[]{:S(2)}) collective-permute-start(f32[1,512]{1,0:T(1,128)S(1)} %get-tuple-element.15), channel_id=1, source_target_pairs={{0,1},{1,0},{2,3},{3,2},{4,5},{5,4},{6,7},{7,6},{8,9},{9,8},{10,11... | collective-permute-start | bytes 6152 | tf_op jit(solution)/shard_map/ppermute | solution.py:454
  121.7 14.7 %collective-permute-start.6 = (f32[1,512]{1,0:T(1,128)S(1)}, f32[1,512]{1,0:T(1,128)S(1)}, u32[]{:S(2)}, u32[]{:S(2)}) collective-permute-start(f32[1,512]{1,0:T(1,128)S(1)} %get-tuple-element.16), channel_id=1, source_target_pairs={{0,1},{1,0},{2,3},{3,2},{4,5},{5,4},{6,7},{7,6},{8,9},{9,8},{10,11... | collective-permute-start | bytes 6152 | tf_op jit(solution)/shard_map/ppermute | solution.py:454
  133.1 8.7 %all-to-all-start.7 = ((f32[4,1,2048]{2,1,0:T(1,128)}), f32[4,1,2048]{2,1,0:T(1,128)S(1)}, u32[]{:S(2)}, u32[]{:S(2)}) async-start(f32[4,1,2048]{2,1,0:T(1,128)} %broadcast_in_dim.100), calls=%async_computation.7 | async-start | bytes 65536 | tf_op jit(solution)/shard_map/all_to_all | solution.py:459
  136.4 14.3 %collective-permute-start.7 = (f32[1,512]{1,0:T(1,128)S(1)}, f32[1,512]{1,0:T(1,128)S(1)}, u32[]{:S(2)}, u32[]{:S(2)}) collective-permute-start(f32[1,512]{1,0:T(1,128)S(1)} %get-tuple-element.28), channel_id=1, source_target_pairs={{0,2},{2,0},{1,3},{3,1},{4,6},{6,4},{5,7},{7,5},{8,10},{10,8},{9,1... | collective-permute-start | bytes 6152 | tf_op jit(solution)/shard_map/ppermute | solution.py:454
  139.9 10.8 %collective-permute-start.5 = (f32[1,512]{1,0:T(1,128)S(1)}, f32[1,512]{1,0:T(1,128)S(1)}, u32[]{:S(2)}, u32[]{:S(2)}) collective-permute-start(f32[1,512]{1,0:T(1,128)S(1)} %get-tuple-element.29), channel_id=1, source_target_pairs={{0,2},{2,0},{1,3},{3,1},{4,6},{6,4},{5,7},{7,5},{8,10},{10,8},{9,1... | collective-permute-start | bytes 6152 | tf_op jit(solution)/shard_map/ppermute | solution.py:454
  150.7 31.3 %collective-permute-start.13 = (f32[1,4096]{1,0:T(1,128)S(1)}, f32[1,4096]{1,0:T(1,128)S(1)}, u32[]{:S(2)}, u32[]{:S(2)}) collective-permute-start(f32[1,4096]{1,0:T(1,128)S(1)} %row_step.4), channel_id=1, source_target_pairs={{0,1},{1,0},{2,3},{3,2},{4,5},{5,4},{6,7},{7,6},{8,9},{9,8},{10,11... | collective-permute-start | bytes 49160 | tf_op jit(solution)/shard_map/ppermute | solution.py:454
  151.4 11.8 %all-to-all-start.2 = ((f32[8,1,512]{2,1,0:T(1,128)}), f32[8,1,512]{2,1,0:T(1,128)S(1)}, u32[]{:S(2)}, u32[]{:S(2)}) async-start(f32[8,1,512]{2,1,0:T(1,128)} %broadcast_in_dim.92), calls=%async_computation.2 | async-start | bytes 32768 | tf_op jit(solution)/shard_map/all_to_all | solution.py:459
  182.9 13.1 %all-to-all-start.8 = ((f32[16,1,4096]{2,1,0:T(1,128)}), f32[16,1,4096]{2,1,0:T(1,128)S(1)}, u32[]{:S(2)}, u32[]{:S(2)}) async-start(f32[16,1,4096]{2,1,0:T(1,128)} %broadcast_in_dim.102), calls=%async_computation.8 | async-start | bytes 524288 | tf_op jit(solution)/shard_map/all_to_all | solution.py:459
  189.9 53.8 %collective-permute-start.8 = (bf16[4096,128]{1,0:T(8,128)(2,1)}, bf16[4096,128]{1,0:T(8,128)(2,1)}, u32[]{:S(2)}, u32[]{:S(2)}) collective-permute-start(bf16[4096,128]{1,0:T(8,128)(2,1)} %constant_dynamic-slice_fusion.5), channel_id=1, source_target_pairs={{0,1},{1,0},{2,3},{3,2},{4,5},{5,4},{6,7},{7,6},{8,9},{9,8},{10,11... | collective-permute-start | bytes 3145736 | tf_op jit(solution)/shard_map/ppermute | solution.py:454
  216.6 22.4 %all-to-all-start.12 = ((bf16[4,512,256]{2,1,0:T(8,128)(2,1)}), bf16[4,512,256]{2,1,0:T(8,128)(2,1)S(1)}, u32[]{:S(2)}, u32[]{:S(2)}) async-start(bf16[4,512,256]{2,1,0:T(8,128)(2,1)} %bitcast.56), calls=%async_computation.12 | async-start | bytes 2097152 | tf_op jit(solution)/shard_map/all_to_all | solution.py:563
  234.5 22.6 %collective-permute-start.15 = (bf16[4096,128]{1,0:T(8,128)(2,1)}, bf16[4096,128]{1,0:T(8,128)(2,1)}, u32[]{:S(2)}, u32[]{:S(2)}) collective-permute-start(bf16[4096,128]{1,0:T(8,128)(2,1)} %constant_dynamic-slice_fusion.2), channel_id=1, source_target_pairs={{0,1},{1,0},{2,3},{3,2},{4,5},{5,4},{6,7},{7,6},{8,9},{9,8},{10,11... | collective-permute-start | bytes 3145736 | tf_op jit(solution)/shard_map/ppermute | solution.py:454
  237.7 1.4 collective-permute-start.14
  240.1 12.7 %all-to-all-start.10 = ((f32[16,1,4096]{2,1,0:T(1,128)}), f32[16,1,4096]{2,1,0:T(1,128)S(1)}, u32[]{:S(2)}, u32[]{:S(2)}) async-start(f32[16,1,4096]{2,1,0:T(1,128)} %broadcast_in_dim.106), calls=%async_computation.10 | async-start | bytes 524288 | tf_op jit(solution)/shard_map/all_to_all | solution.py:459
  243.6 13.4 %copy-start.8 = (bf16[8,512,256]{2,1,0:T(8,128)(2,1)S(1)}, bf16[8,512,256]{2,1,0:T(8,128)(2,1)}, u32[]{:S(2)}) copy-start(bf16[8,512,256]{2,1,0:T(8,128)(2,1)} %copy-done.7) | copy-start | bytes 6291460
  252.8 18.8 %all-to-all-start.3 = ((bf16[4,1024,128]{2,1,0:T(8,128)(2,1)}), bf16[4,1024,128]{2,1,0:T(8,128)(2,1)}, u32[]{:S(2)}, u32[]{:S(2)}) async-start(bf16[4,1024,128]{2,1,0:T(8,128)(2,1)} %bitcast.61), calls=%async_computation.3 | async-start | bytes 2097152 | tf_op jit(solution)/shard_map/all_to_all | solution.py:479
  271.6 17.4 %all-to-all-start.11 = ((bf16[4,1024,128]{2,1,0:T(8,128)(2,1)}), bf16[4,1024,128]{2,1,0:T(8,128)(2,1)S(1)}, u32[]{:S(2)}, u32[]{:S(2)}) async-start(bf16[4,1024,128]{2,1,0:T(8,128)(2,1)} %bitcast.60), calls=%async_computation.11 | async-start | bytes 2097152 | tf_op jit(solution)/shard_map/all_to_all | solution.py:479
  288.9 19.5 %all-to-all-start.13 = ((bf16[4,512,256]{2,1,0:T(8,128)(2,1)}), bf16[4,512,256]{2,1,0:T(8,128)(2,1)}, u32[]{:S(2)}, u32[]{:S(2)}) async-start(bf16[4,512,256]{2,1,0:T(8,128)(2,1)} %bitcast.28), calls=%async_computation.13 | async-start | bytes 2097152 | tf_op jit(solution)/shard_map/all_to_all | solution.py:564
  300.8 9.1 %collective-permute-start.9 = (bf16[512,128]{1,0:T(8,128)(2,1)S(1)}, bf16[512,128]{1,0:T(8,128)(2,1)S(1)}, u32[]{:S(2)}, u32[]{:S(2)}) collective-permute-start(bf16[512,128]{1,0:T(8,128)(2,1)S(1)} %constant_dynamic-slice_fusion.4), channel_id=1, source_target_pairs={{0,16},{16,0},{1,17},{17,1},{2,18},{18,2},{3,19},{19,3},{4,20},{20... | collective-permute-start | bytes 393224 | tf_op jit(solution)/shard_map/ppermute | solution.py:454
  301.6 8.4 %collective-permute-start.16 = (bf16[512,128]{1,0:T(8,128)(2,1)S(1)}, bf16[512,128]{1,0:T(8,128)(2,1)S(1)}, u32[]{:S(2)}, u32[]{:S(2)}) collective-permute-start(bf16[512,128]{1,0:T(8,128)(2,1)S(1)} %constant_dynamic-slice_fusion.1), channel_id=1, source_target_pairs={{0,16},{16,0},{1,17},{17,1},{2,18},{18,2},{3,19},{19,3},{4,20},{20... | collective-permute-start | bytes 393224 | tf_op jit(solution)/shard_map/ppermute | solution.py:454
  310.5 5.8 %collective-permute-start.17 = (bf16[256,128]{0,1:T(8,128)(2,1)S(1)}, bf16[256,128]{0,1:T(8,128)(2,1)S(1)}, u32[]{:S(2)}, u32[]{:S(2)}) collective-permute-start(bf16[256,128]{0,1:T(8,128)(2,1)S(1)} %dynamic-slice_convert_fusion), channel_id=1, source_target_pairs={{0,2},{2,0},{1,3},{3,1},{4,6},{6,4},{5,7},{7,5},{8,10},{10,8},{9,1... | collective-permute-start | bytes 196616 | tf_op jit(solution)/shard_map/ppermute | solution.py:454
  316.4 1.3 collective-permute-start.18
  (16 other events, 63.9 us)
